TPU v7x, 512 devices: a whole 4x4x16 slice. The times are simulated.
512 devices in a mesh: rows: 16 (over z_hi, x, core), labels: 32 (over y, z_lo).
Axes of the slice: x: 4, y: 4, z: 16 (z_hi: 2, z_lo: 8; z = z_hi * 8 + z_lo), core: 2. Of those that a mesh axis runs over, the one named last changes fastest.
Arguments:
- pool_features: bfloat16 [2048, 768], P('rows'), may hold values from -6 to 6
- pool_labels: int32 [2048, 16], P('rows'), may hold values from 0 to 196607
- pool_counts: int32 [2048], P('rows'), may hold values from 1 to 16
- batch_rows: int32 [2, 512], P(None, 'rows'), may hold values from 0 to 127
- weights: float32 [196608, 768], P(('rows', 'labels')), may hold values from -0.21875 to 0.21875
- momentum: float32 [196608, 768], P(('rows', 'labels')), may hold values from -24 to 24
Outputs:
- new_weights: float32 [196608, 768], P(('rows', 'labels'))
- new_momentum: float32 [196608, 768], P(('rows', 'labels'))
- feature_grads: float32 [2, 512, 768], P(None, 'rows')
Inputs may be any that keep to these rules, and one draw needn't show every extreme that they name: `pool_labels`: slots of a list at or past its count are padding and are ignored; a label may appear twice in a list. `batch_rows`: an entry names one of the 128 examples stored with the index of rows that owns that batch row.
All inputs are finite; a program needn't handle non-finite values.
Results may differ from a plain program's by a relative error of at most 0.00045.
The roundings to bfloat16 on the way count: a program that leaves them out, or rounds other values in their place, can miss the bound.
Values may be sent and summed in bfloat16 or wider, within the bound.
A program may use at most 64 MiB of HBM per device.

v0:
```python
import math
import jax
import jax.numpy as jnp
from jax import lax
from jax.sharding import PartitionSpec as P

learn_rate = 0.001
decay_rate = 0.9


def side_by_side(arrays, axis, dim, along):
    widths = [math.prod(a.shape[along:]) for a in arrays]
    both = jnp.concatenate(
        [a.reshape(*a.shape[:along], w) for a, w in zip(arrays, widths)], axis=along
    )
    filled = lax.all_gather(both, axis, axis=dim, tiled=True)
    tiles = jnp.split(filled, [sum(widths[:k]) for k in range(1, len(widths))], axis=along)
    return tuple(
        (b.reshape(*filled.shape[:along], *a.shape[along:]) for a, b in zip(arrays, tiles))
    )


def feature_sums(errors_list, lowered_list, group_rows, width):
    parts = []
    for errors, low_weights in zip(errors_list, lowered_list):
        parts.append(jnp.dot(errors, low_weights, preferred_element_type=jnp.float32))
    whole = lax.psum(jnp.concatenate(parts, axis=1), ("rows", "labels"))
    mine = lax.dynamic_slice_in_dim(whole, lax.axis_index("rows") * group_rows, group_rows, 0)
    return jnp.stack([mine[:, :width], mine[:, width:]])


def per_device(pool_features, pool_labels, pool_counts, batch_rows, weights, momentum):
    lab_rows = weights.shape[0]
    group_rows = batch_rows.shape[1]
    width = weights.shape[1]
    device_index = lax.axis_index("rows") * lax.axis_size("labels") + lax.axis_index("labels")
    labels = device_index * lab_rows + jnp.arange(lab_rows, dtype=jnp.int32)
    all_ids, all_counts = side_by_side(
        (pool_labels[batch_rows], pool_counts[batch_rows]), "rows", 1, 2
    )
    all_features = lax.all_gather(pool_features[batch_rows], "rows", axis=1, tiled=True)
    errors_list = []
    lowered_list = []
    for batch in range(2):
        features = all_features[batch]
        label_ids = all_ids[batch]
        in_list = (
            jnp.arange(label_ids.shape[1], dtype=jnp.int32)[None, :] < all_counts[batch][:, None]
        )
        matched = (label_ids[:, :, None] == labels[None, None, :]) & in_list[:, :, None]
        targets = jnp.any(matched, axis=1).astype(jnp.float32)
        low_weights = weights.astype(jnp.bfloat16)
        logits = lax.dot_general(
            features, low_weights, (((1,), (1,)), ((), ())), preferred_element_type=jnp.float32
        )
        errors = (jax.nn.sigmoid(logits) - targets).astype(jnp.bfloat16)
        grads = lax.dot_general(
            errors, features, (((0,), (0,)), ((), ())), preferred_element_type=jnp.float32
        )
        errors_list.append(errors)
        lowered_list.append(low_weights)
        momentum = decay_rate * momentum + grads
        weights = weights - learn_rate * momentum
    return (weights, momentum, feature_sums(errors_list, lowered_list, group_rows, width))


def solution(mesh):
    in_specs = (
        P("rows", None),
        P("rows", None),
        P("rows"),
        P(None, "rows"),
        P(("rows", "labels"), None),
        P(("rows", "labels"), None),
    )
    out_specs = (P(("rows", "labels"), None), P(("rows", "labels"), None), P(None, "rows", None))
    return jax.shard_map(
        per_device, mesh=mesh, in_specs=in_specs, out_specs=out_specs, check_vma=False
    )
```

profile of v0, /device:TPU:2, one launch (start us, length us, event | category | flops | bytes accessed | tf_op | source)
XLA Modules:
  0.0 595.8 jit_solution(10529048860126078827)
XLA Ops:
  7.2 0.0 all-gather.3.cloned.1.call-start
  7.2 0.7 compare_select_fusion
  8.0 0.1 reshape.71
  8.1 0.0 copy-done
  8.1 1.3 gather_fusion
  9.4 0.0 all-gather.3.cloned.1.call-update
  9.5 0.0 all-reduce.2.cloned.1.call-start
  9.5 0.8 gather_fusion.2
  10.3 0.1 reshape.68
  10.4 0.1 copy.21
  10.5 0.1 copy.19
  10.6 0.6 gather_fusion.1
  11.2 0.1 pad_add_fusion
  11.4 46.1 %all_gather.7 = s32[2,512,17]{2,0,1:T(2,128)S(1)} all-gather(s32[2,32,17]{2,0,1:T(2,128)S(1)} %pad_add_fusion), channel_id=1, replica_groups=mesh['rows'=16,'labels'=32] {'rows'}, dimensions={1}, use_global_device_ids=true | all-gather | bytes 73984 | tf_op jit(solution)/shard_map/all_gather | solution.py:16
  57.4 19.6 %slice_reduce_fusion = (s32[512]{0:T(512)S(1)}, s32[512]{0:T(512)S(1)}) fusion(s32[2,512,17]{2,0,1:T(2,128)S(1)} %all_gather.7), kind=kLoop, calls=%fused_computation.28 | loop fusion | bytes 8192 | tf_op jit(solution)/shard_map/slice | solution.py:48
  77.1 0.2 iota_compare_fusion
  77.3 0.4 fusion.14
  77.7 8.2 %and_reduce_fusion = (pred[512,384]{1,0:T(8,128)(4,1)S(1)}, pred[512,384]{1,0:T(8,128)(4,1)S(1)}) fusion(s32[512,16]{1,0:T(8,128)S(1)} %bitcast.27, s32[384]{0:T(512)S(1)} %iota_add_fusion, pred[512,16]{1,0:T(8,128)(4,1)S(1)} %get-tuple-element.15, pred[512,16]{1,0:T(8,128)(4,1)S(1)} %get-tuple-element.16, s32[512,16]{1,0:T(8,128)S(1)} %bitcast.26), kind=kLoop, calls=%fused_computation.3 | loop fusion | flops 18481152 | bytes 476672 | tf_op jit(solution)/shard_map/reduce_or | solution.py:51
  85.9 17.5 %all-gather.3.cloned.1.call-done = bf16[2,512,768]{2,1,0:T(8,128)(2,1)} async-done(((bf16[2,32,768]{2,1,0:T(8,128)(2,1)}), bf16[2,512,768]{2,1,0:T(8,128)(2,1)}) %all-gather.3.cloned.1.call-update) | async-done | bytes 1572880 | tf_op jit(solution)/shard_map/all_gather | solution.py:41
  103.4 1.8 fusion.9
  105.2 0.6 fusion.11
  105.8 0.8 copy-done.3
  106.6 0.3 copy-done.4
  106.9 0.6 fusion.10
  107.5 0.7 fusion.8
  108.1 0.6 fusion.15
  108.7 2.1 pad_maximum_fusion
  110.8 0.0 all-reduce.2.cloned.1.call-update
  110.8 3.2 multiply_subtract_fusion
  113.9 473.3 %all-reduce.2.cloned.1.call-done = f32[512,1536]{1,0:T(8,128)} async-done(((f32[512,1536]{1,0:T(8,128)}), f32[512,1536]{1,0:T(8,128)}) %all-reduce.2.cloned.1.call-update) | async-done | bytes 3145744 | tf_op jit(solution)/shard_map/psum | solution.py:27
  587.3 1.0 dynamic-slice_bitcast_fusion.1
  588.2 0.7 pad_maximum_fusion.1
  (12 shorter events, 0.1 us)
Async XLA Ops:
  7.2 0.9 copy-start
  7.2 2.3 copy-start.1
  7.2 3.3 copy-start.5
  7.2 96.2 %all-gather.3.cloned.1.call-start = ((), (), s32[]{:S(2)}) async-start(), calls=%async_computation.1 | async-start | bytes 1671168 | tf_op jit(solution)/shard_map/all_gather | solution.py:41
  9.5 577.8 %all-reduce.2.cloned.1.call-start = ((), (), s32[]{:S(2)}) async-start(), calls=%async_computation | async-start | bytes 6291456 | tf_op jit(solution)/shard_map/psum | solution.py:27
  11.4 92.0 %copy-start.2 = (f32[384,768]{1,0:T(8,128)S(1)}, f32[384,768]{1,0:T(8,128)}, u32[]{:S(2)}) copy-start(f32[384,768]{1,0:T(8,128)} %param.10) | copy-start | bytes 3538948
  105.2 1.4 copy-start.3
  105.2 1.7 copy-start.4
Sparse Core Ops, SparseCore 0:
  12.0 91.3 all-gather.2
  110.9 476.3 all-reduce.1
where the time goes:
time: 596 us
  waiting for transfers between devices  491 us (82%)
  blocking collectives  46.1 us (8%)
  local copies, waits for them, and re-layouts  25.3 us (4%)
  between operations  14.2 us (2%)
  other arithmetic  12 us (2%)
  matrix products  7.3 us (1%)
    psum x1, waiting for transfers between devices, feature_sums(): whole = lax.psum(jnp.concatenate(parts, axis=1), ('rows', 'labels'))  473 us
    all_gather x1, blocking collectives, side_by_side(): filled = lax.all_gather(both, axis, axis=dim, tiled=True)  46.1 us
    slice x1, local copies, waits for them, and re-layouts, per_device(): all_counts[batch][:, None]  19.6 us
    all_gather x1, waiting for transfers between devices, per_device(): lax.all_gather(pool_features[batch_rows], 'rows', axis=1, tiled=True)  17.5 us
  transfers between devices with their start and end apart: 2, of which 2 were waited for; matrix products, arithmetic and copies ran while one was open for 6% of the time, Pallas kernels for 0%

commit v1 on v0

--- a/solution.py
+++ b/solution.py
@@ -24,7 +24,9 @@
     parts = []
     for errors, low_weights in zip(errors_list, lowered_list):
         parts.append(jnp.dot(errors, low_weights, preferred_element_type=jnp.float32))
-    whole = lax.psum(jnp.concatenate(parts, axis=1), ("rows", "labels"))
+    whole = jnp.concatenate(parts, axis=1)
+    for mesh_axis in ("rows", "labels"):
+        whole = lax.psum(whole, mesh_axis)
     mine = lax.dynamic_slice_in_dim(whole, lax.axis_index("rows") * group_rows, group_rows, 0)
     return jnp.stack([mine[:, :width], mine[:, width:]])
 

time: 596 us -> 882 us (1.48)
  the two profiles are of different devices: /device:TPU:2 before, /device:TPU:34 now
where the time goes in v1:
time: 882 us
  waiting for transfers between devices  783 us (89%)
  blocking collectives  40.8 us (5%)
  local copies, waits for them, and re-layouts  25.3 us (3%)
  between operations  13.9 us (2%)
  other arithmetic  12 us (1%)
    psum x2, waiting for transfers between devices, feature_sums(): whole = lax.psum(whole, mesh_axis)  766 us
    all_gather x1, blocking collectives, side_by_side(): filled = lax.all_gather(both, axis, axis=dim, tiled=True)  40.8 us
    slice x1, local copies, waits for them, and re-layouts, per_device(): all_counts[batch][:, None]  19.6 us
  transfers between devices with their start and end apart: 3, of which 3 were waited for; matrix products, arithmetic and copies ran while one was open for 4% of the time, Pallas kernels for 0%

profile of v1, /device:TPU:34, one launch (start us, length us, event | category | flops | bytes accessed | tf_op | source)
XLA Modules:
  0.0 882.1 jit_solution(3548688595397934338)
XLA Ops:
  7.2 0.0 all-gather.3.cloned.1.call-start
  7.2 0.7 compare_select_fusion
  8.0 0.1 reshape.71
  8.1 0.0 copy-done
  8.1 1.3 gather_fusion
  9.5 0.0 all-reduce.3.cloned.1.call-start
  9.5 0.8 gather_fusion.2
  10.3 0.1 reshape.68
  10.4 0.1 copy.21
  10.5 0.1 copy.19
  10.6 0.6 gather_fusion.1
  11.2 0.1 pad_add_fusion
  11.4 40.8 %all_gather.7 = s32[2,512,17]{2,0,1:T(2,128)S(1)} all-gather(s32[2,32,17]{2,0,1:T(2,128)S(1)} %pad_add_fusion), channel_id=1, replica_groups=mesh['rows'=16,'labels'=32] {'rows'}, dimensions={1}, use_global_device_ids=true | all-gather | bytes 73984 | tf_op jit(solution)/shard_map/all_gather | solution.py:16
  52.2 19.6 %slice_reduce_fusion = (s32[512]{0:T(512)S(1)}, s32[512]{0:T(512)S(1)}) fusion(s32[2,512,17]{2,0,1:T(2,128)S(1)} %all_gather.7), kind=kLoop, calls=%fused_computation.28 | loop fusion | bytes 8192 | tf_op jit(solution)/shard_map/slice | solution.py:50
  71.8 0.2 iota_compare_fusion
  72.0 0.4 fusion.14
  72.4 8.2 and_reduce_fusion
  80.6 17.1 %all-gather.3.cloned.1.call-done = bf16[2,512,768]{2,1,0:T(8,128)(2,1)} async-done(((bf16[2,32,768]{2,1,0:T(8,128)(2,1)}), bf16[2,512,768]{2,1,0:T(8,128)(2,1)}) %all-gather.3.cloned.1.call-update) | async-done | bytes 1572880 | tf_op jit(solution)/shard_map/all_gather | solution.py:43
  97.7 1.8 fusion.9
  99.6 0.6 fusion.11
  100.1 0.8 copy-done.3
  101.0 0.3 copy-done.4
  101.3 0.6 fusion.10
  101.9 0.7 fusion.8
  102.5 0.6 fusion.15
  103.1 2.1 pad_maximum_fusion
  105.2 0.0 all-reduce.5.cloned.1.call-start
  105.2 283.0 %all-reduce.3.cloned.1.call-done = f32[512,1536]{1,0:T(8,128)} async-done(((f32[512,1536]{1,0:T(8,128)}), f32[512,1536]{1,0:T(8,128)}) %all-reduce.3.cloned.1.call-update) | async-done | bytes 3145744 | tf_op jit(solution)/shard_map/psum | solution.py:29
  388.2 3.2 multiply_subtract_fusion
  391.4 482.5 %all-reduce.5.cloned.1.call-done = f32[512,1536]{1,0:T(8,128)} async-done(((f32[512,1536]{1,0:T(8,128)}), f32[512,1536]{1,0:T(8,128)}) %all-reduce.5.cloned.1.call-update) | async-done | bytes 3145744 | tf_op jit(solution)/shard_map/psum | solution.py:29
  873.9 1.0 dynamic-slice_bitcast_fusion.1
  874.9 0.7 pad_maximum_fusion.1
  (15 shorter events, 0.1 us)
Async XLA Ops:
  7.2 0.9 copy-start
  7.2 2.3 copy-start.1
  7.2 3.3 copy-start.5
  7.2 90.5 %all-gather.3.cloned.1.call-start = ((), (), s32[]{:S(2)}) async-start(), calls=%async_computation.2 | async-start | bytes 1671168 | tf_op jit(solution)/shard_map/all_gather | solution.py:43
  9.5 378.7 %all-reduce.3.cloned.1.call-start = ((), (), s32[]{:S(2)}) async-start(), calls=%async_computation | async-start | bytes 6291456 | tf_op jit(solution)/shard_map/psum | solution.py:29
  11.4 86.4 %copy-start.2 = (f32[384,768]{1,0:T(8,128)S(1)}, f32[384,768]{1,0:T(8,128)}, u32[]{:S(2)}) copy-start(f32[384,768]{1,0:T(8,128)} %param.10) | copy-start | bytes 3538948
  99.5 1.4 copy-start.3
  99.6 1.7 copy-start.4
  105.2 768.7 %all-reduce.5.cloned.1.call-start = ((), (), s32[]{:S(2)}) async-start(), calls=%async_computation.1 | async-start | bytes 6291456 | tf_op jit(solution)/shard_map/psum | solution.py:29
Sparse Core Ops, SparseCore 0:
  12.0 85.7 all-gather.2
  105.3 282.8 all-reduce.2
  391.1 482.7 all-reduce.4
